TPU v7x, 32 devices: a whole 2x2x4 slice. The times are simulated.
32 devices in a mesh: rep: 8 (over y, x, core), shard: 4 (over z).
Axes of the slice: x: 2, y: 2, z: 4, core: 2. Of those that a mesh axis runs over, the one named last changes fastest.
Arguments:
- prompt_x: bfloat16 [8, 8, 2048, 800], P(None, 'rep', 'shard'), may hold values from -6 to 6
- cont_x: bfloat16 [8, 32, 512, 800], P(None, ('rep', 'shard')), may hold values from -6 to 6
- cont_map: int32 [8, 32, 2], P(None, ('rep', 'shard')), may hold values from 0 to 7
- cont_start: int32 [8, 32, 2], P(None, ('rep', 'shard')), may hold values from 0 to 511, as said below
- w_in: float32 [800, 400], P('shard'), may hold values from -0.21875 to 0.21875
- w_conv: float32 [3, 400, 400], P(None, 'shard'), may hold values from -0.1875 to 0.1875
- w_out: float32 [400, 800], P('shard'), may hold values from -0.4375 to 0.4375
- norm1_gain: float32 [800], replicated, may hold values from 0.1 to 1.9
- norm1_bias: float32 [800], replicated, may hold values from -3 to 3
- bias_in: float32 [400], replicated, may hold values from -3 to 3
- norm2_gain: float32 [400], replicated, may hold values from 0.1 to 1.9
- norm2_bias: float32 [400], replicated, may hold values from -3 to 3
- bias_conv: float32 [400], replicated, may hold values from -3 to 3
- norm3_gain: float32 [400], replicated, may hold values from 0.1 to 1.9
- norm3_bias: float32 [400], replicated, may hold values from -3 to 3
- bias_out: float32 [800], replicated, may hold values from -3 to 3
- prompt_cot: bfloat16 [8, 8, 2048, 800], P(None, 'rep', 'shard'), may hold values from -6 to 6
- cont_cot: bfloat16 [8, 32, 512, 800], P(None, ('rep', 'shard')), may hold values from -6 to 6
Outputs:
- prompt_out: bfloat16 [8, 8, 2048, 800], P(None, 'rep', 'shard')
- cont_out: bfloat16 [8, 32, 512, 800], P(None, ('rep', 'shard'))
- prompt_grad: float32 [8, 8, 2048, 800], P(None, 'rep', 'shard')
- cont_grad: float32 [8, 32, 512, 800], P(None, ('rep', 'shard'))
- grad_w_in: float32 [800, 400], P('shard')
- grad_w_conv: float32 [3, 400, 400], P(None, 'shard')
- grad_w_out: float32 [400, 800], P('shard')
- grad_norm1_gain: float32 [800], replicated
- grad_norm1_bias: float32 [800], replicated
- grad_bias_in: float32 [400], replicated
- grad_norm2_gain: float32 [400], replicated
- grad_norm2_bias: float32 [400], replicated
- grad_bias_conv: float32 [400], replicated
- grad_norm3_gain: float32 [400], replicated
- grad_norm3_bias: float32 [400], replicated
- grad_bias_out: float32 [800], replicated
Inputs may be any that keep to these rules, and one draw needn't show every extreme that they name: `cont_start`: in each buffer the 2 starts rise strictly and the first is 0; a continuation runs from its start to the next start or to the buffer's end. In the first buffer of every micro-batch the last start is 511.
All inputs are finite; a program needn't handle non-finite values.
Results may differ from a plain program's by a relative error of at most 0.0099.
Values may be sent and summed in bfloat16 or wider, within the bound.
No kernel may reach another device: no remote copies, remote signals or barrier semaphores. Data moves between devices by JAX's collectives and lax.ppermute only.
A program may use at most 256 MiB of HBM per device.

v0:
```python
import jax
import jax.numpy as jnp
from jax import lax
from jax.sharding import PartitionSpec as P

DILATION_STEP = 16
epsilon = 1e-05


def passed_along(x, axis, by):
    size = lax.axis_size(axis)
    pairs = [(i, i + by) for i in range(size) if 0 <= i + by < size]
    return lax.ppermute(x, axis, pairs)


def from_root(value, axis, source):
    kept = jnp.where(lax.axis_index(axis) == source, value, 0).astype(value.dtype)
    return lax.psum(kept, axis)


def norm_forward(values, gain, shift_by):
    center = values - jnp.mean(values, axis=-1, keepdims=True)
    scale = lax.rsqrt(jnp.mean(center * center, axis=-1, keepdims=True) + epsilon)
    normed = center * scale
    return (normed * gain + shift_by, normed, scale)


def norm_backward(grad, normed, scale, gain):
    scaled = grad * gain
    return scale * (
        scaled
        - jnp.mean(scaled, axis=-1, keepdims=True)
        - normed * jnp.mean(scaled * normed, axis=-1, keepdims=True)
    )


def silu_slope(values):
    sigma = jax.nn.sigmoid(values)
    return sigma * (1.0 + values * (1.0 - sigma))


def row_total(values):
    return jnp.sum(values, axis=(0, 1))


def layout(cont_start, cont_map, continuation_row_block, receptive_width):
    starts = cont_start[:, 0]
    owners = cont_map[:, 0]
    row_ids = jnp.arange(continuation_row_block, dtype=jnp.int32)
    member = jnp.sum((row_ids[None, :, None] >= starts[:, None, :]).astype(jnp.int32), axis=-1) - 1
    picked = member[:, :, None] == jnp.arange(starts.shape[1], dtype=jnp.int32)[None, None, :]
    begin = jnp.sum(jnp.where(picked, starts[:, None, :], 0), axis=-1)
    owning_prompt = jnp.sum(jnp.where(picked, owners[:, None, :], 0), axis=-1)
    row_position = row_ids[None, :] - begin
    causal_masks = [
        row_position >= kernel_tap_index * DILATION_STEP for kernel_tap_index in range(3)
    ]
    indices = [
        owning_prompt * receptive_width
        + jnp.clip(
            receptive_width + row_position - kernel_tap_index * DILATION_STEP,
            0,
            receptive_width - 1,
        )
        for kernel_tap_index in range(3)
    ]
    return (causal_masks, indices)


def pick_rows(table, row_index):
    return jax.vmap(lambda block, where_from: block[where_from])(table, row_index)


def on_device(
    prompt_x,
    cont_x,
    cont_map,
    cont_start,
    w_in,
    w_conv,
    w_out,
    norm1_gain,
    norm1_bias,
    bias_in,
    norm2_gain,
    norm2_bias,
    bias_conv,
    norm3_gain,
    norm3_bias,
    bias_out,
    prompt_cot,
    cont_cot,
):
    receptive_width = 2 * DILATION_STEP
    inner = w_conv.shape[2]
    prompt_row_block = prompt_x.shape[2]
    continuation_row_block = cont_x.shape[2]
    batches = prompt_x.shape[0]
    last_shard = lax.axis_size("shard") - 1
    low_in, low_conv, low_out = (
        lax.all_gather(w_in.astype(jnp.bfloat16), "shard", axis=0, tiled=True),
        lax.all_gather(w_conv.astype(jnp.bfloat16), "shard", axis=1, tiled=True),
        lax.all_gather(w_out.astype(jnp.bfloat16), "shard", axis=0, tiled=True),
    )
    rows_in = jnp.concatenate([prompt_x[:, 0], cont_x[:, 0]], axis=1).astype(jnp.float32)
    pre_one, normed_one, scale_one = norm_forward(rows_in, norm1_gain, norm1_bias)
    act_in = jax.nn.silu(pre_one).astype(jnp.bfloat16)
    hidden_in = (
        jnp.einsum("mrd,de->mre", act_in, low_in, preferred_element_type=jnp.float32) + bias_in
    )
    pre_two, normed_two, scale_two = norm_forward(hidden_in, norm2_gain, norm2_bias)
    act_mid = jax.nn.silu(pre_two).astype(jnp.bfloat16)
    prompt_act = act_mid[:, :prompt_row_block]
    cont_act = act_mid[:, prompt_row_block:]
    rim_rows = prompt_act[:, prompt_row_block - receptive_width :]
    halo_rows = passed_along(rim_rows, "shard", 1)
    tail_here = from_root(rim_rows, "shard", last_shard)
    tails = lax.all_gather(tail_here, "rep", axis=1, tiled=True)
    table_rows = tails.shape[1]
    causal_masks, indices = layout(cont_start, cont_map, continuation_row_block, receptive_width)
    widened_input = jnp.concatenate([halo_rows, prompt_act], axis=1)
    prompt_kernel_taps = jnp.concatenate(
        [
            widened_input[
                :,
                receptive_width
                - kernel_tap_index * DILATION_STEP : receptive_width
                - kernel_tap_index * DILATION_STEP
                + prompt_row_block,
            ]
            for kernel_tap_index in range(3)
        ],
        axis=-1,
    )
    widened_continuation = jnp.concatenate(
        [jnp.zeros((batches, receptive_width, inner), jnp.bfloat16), cont_act], axis=1
    )
    cont_pieces = []
    for kernel_tap_index in range(3):
        nearby_rows = widened_continuation[
            :,
            receptive_width
            - kernel_tap_index * DILATION_STEP : receptive_width
            - kernel_tap_index * DILATION_STEP
            + continuation_row_block,
        ]
        if kernel_tap_index == 0:
            cont_pieces.append(nearby_rows)
        else:
            distant_rows = pick_rows(tails, indices[kernel_tap_index])
            cont_pieces.append(
                jnp.where(causal_masks[kernel_tap_index][..., None], nearby_rows, distant_rows)
            )
    taps = jnp.concatenate([prompt_kernel_taps, jnp.concatenate(cont_pieces, axis=-1)], axis=1)
    conv_flat = low_conv.reshape(3 * inner, inner)
    conv_out = (
        jnp.einsum("mrk,ke->mre", taps, conv_flat, preferred_element_type=jnp.float32) + bias_conv
    )
    pre_three, normed_three, scale_three = norm_forward(conv_out, norm3_gain, norm3_bias)
    act_conv = jax.nn.silu(pre_three).astype(jnp.bfloat16)
    branch_out = (
        jnp.einsum("mri,id->mrd", act_conv, low_out, preferred_element_type=jnp.float32) + bias_out
    )
    block_out = (rows_in + branch_out).astype(jnp.bfloat16)
    back_in, back_conv, back_out = (
        lax.all_gather(w_in.astype(jnp.bfloat16), "shard", axis=0, tiled=True),
        lax.all_gather(w_conv.astype(jnp.bfloat16), "shard", axis=1, tiled=True),
        lax.all_gather(w_out.astype(jnp.bfloat16), "shard", axis=0, tiled=True),
    )
    grad_low = jnp.concatenate([prompt_cot[:, 0], cont_cot[:, 0]], axis=1)
    grad_rows = grad_low.astype(jnp.float32)
    part_bias_out = row_total(grad_rows)
    full_w_out = jnp.einsum("mri,mrd->id", act_conv, grad_low, preferred_element_type=jnp.float32)
    grad_act_conv = jnp.einsum(
        "mrd,id->mri", grad_low, back_out, preferred_element_type=jnp.float32
    )
    grad_act_conv = grad_act_conv * silu_slope(pre_three)
    part_gain_three = row_total(grad_act_conv * normed_three)
    part_shift_three = row_total(grad_act_conv)
    grad_conv_out = norm_backward(grad_act_conv, normed_three, scale_three, norm3_gain)
    part_bias_conv = row_total(grad_conv_out)
    grad_conv_low = grad_conv_out.astype(jnp.bfloat16)
    full_w_conv = jnp.einsum(
        "mrk,mre->ke", taps, grad_conv_low, preferred_element_type=jnp.float32
    ).reshape(3, inner, inner)
    grad_taps = jnp.einsum(
        "mre,ke->mrk",
        grad_conv_low,
        back_conv.reshape(3 * inner, inner),
        preferred_element_type=jnp.float32,
    )
    grad_extended = 0.0
    grad_extended_cont = 0.0
    tail_part = jnp.zeros((batches, table_rows, inner), jnp.float32)
    for kernel_tap_index in range(3):
        prompt_portion = grad_taps[
            :, :prompt_row_block, kernel_tap_index * inner : (kernel_tap_index + 1) * inner
        ]
        grad_extended = grad_extended + jnp.pad(
            prompt_portion,
            (
                (0, 0),
                (
                    receptive_width - kernel_tap_index * DILATION_STEP,
                    kernel_tap_index * DILATION_STEP,
                ),
                (0, 0),
            ),
        )
        cont_piece = grad_taps[
            :, prompt_row_block:, kernel_tap_index * inner : (kernel_tap_index + 1) * inner
        ]
        keep_near = causal_masks[kernel_tap_index][..., None]
        grad_extended_cont = grad_extended_cont + jnp.pad(
            jnp.where(keep_near, cont_piece, 0.0),
            (
                (0, 0),
                (
                    receptive_width - kernel_tap_index * DILATION_STEP,
                    kernel_tap_index * DILATION_STEP,
                ),
                (0, 0),
            ),
        )
        if kernel_tap_index > 0:
            far_piece = jnp.where(keep_near, 0.0, cont_piece)
            tail_part = tail_part + jax.vmap(
                lambda values, where_to: jax.ops.segment_sum(
                    values, where_to, num_segments=table_rows
                )
            )(far_piece, indices[kernel_tap_index])
    back_rim = passed_along(
        grad_extended[:, :receptive_width].astype(jnp.bfloat16), "shard", -1
    ).astype(jnp.float32)
    tail_total, grad_bias_conv, grad_norm3_gain, grad_norm3_bias, grad_bias_out = lax.psum(
        (tail_part, part_bias_conv, part_gain_three, part_shift_three, part_bias_out),
        ("rep", "shard"),
    )
    own_tail = lax.dynamic_slice_in_dim(
        tail_total, lax.axis_index("rep") * receptive_width, receptive_width, 1
    )
    rim_grad = back_rim + jnp.where(lax.axis_index("shard") == last_shard, own_tail, 0.0)
    grad_prompt_act = grad_extended[:, receptive_width:]
    grad_prompt_act = jnp.concatenate(
        [
            grad_prompt_act[:, : prompt_row_block - receptive_width],
            grad_prompt_act[:, prompt_row_block - receptive_width :] + rim_grad,
        ],
        axis=1,
    )
    grad_act_mid = jnp.concatenate(
        [grad_prompt_act, grad_extended_cont[:, receptive_width:]], axis=1
    )
    grad_act_mid = grad_act_mid * silu_slope(pre_two)
    part_gain_two = row_total(grad_act_mid * normed_two)
    part_shift_two = row_total(grad_act_mid)
    grad_hidden = norm_backward(grad_act_mid, normed_two, scale_two, norm2_gain)
    part_bias_in = row_total(grad_hidden)
    grad_hidden_low = grad_hidden.astype(jnp.bfloat16)
    full_w_in = jnp.einsum(
        "mrd,mre->de", act_in, grad_hidden_low, preferred_element_type=jnp.float32
    )
    grad_act_in = jnp.einsum(
        "mre,de->mrd", grad_hidden_low, back_in, preferred_element_type=jnp.float32
    )
    grad_act_in = grad_act_in * silu_slope(pre_one)
    part_gain_one = row_total(grad_act_in * normed_one)
    part_shift_one = row_total(grad_act_in)
    grad_inputs = grad_rows + norm_backward(grad_act_in, normed_one, scale_one, norm1_gain)
    grad_norm1_gain, grad_norm1_bias, grad_bias_in, grad_norm2_gain, grad_norm2_bias = lax.psum(
        (part_gain_one, part_shift_one, part_bias_in, part_gain_two, part_shift_two),
        ("rep", "shard"),
    )
    owned_in, owned_conv, owned_out = (
        lax.psum_scatter(full_w_in, "shard", scatter_dimension=0, tiled=True),
        lax.psum_scatter(full_w_conv, "shard", scatter_dimension=1, tiled=True),
        lax.psum_scatter(full_w_out, "shard", scatter_dimension=0, tiled=True),
    )
    grad_w_in, grad_w_conv, grad_w_out = lax.psum((owned_in, owned_conv, owned_out), "rep")
    prompt_out = block_out[:, None, :prompt_row_block]
    cont_out = block_out[:, None, prompt_row_block:]
    prompt_grad = grad_inputs[:, None, :prompt_row_block]
    cont_grad = grad_inputs[:, None, prompt_row_block:]
    return (
        prompt_out,
        cont_out,
        prompt_grad,
        cont_grad,
        grad_w_in,
        grad_w_conv,
        grad_w_out,
        grad_norm1_gain,
        grad_norm1_bias,
        grad_bias_in,
        grad_norm2_gain,
        grad_norm2_bias,
        grad_bias_conv,
        grad_norm3_gain,
        grad_norm3_bias,
        grad_bias_out,
    )


def solution(mesh):
    in_specs = (
        P(None, "rep", "shard", None),
        P(None, ("rep", "shard"), None, None),
        P(None, ("rep", "shard"), None),
        P(None, ("rep", "shard"), None),
        P("shard", None),
        P(None, "shard", None),
        P("shard", None),
        P(),
        P(),
        P(),
        P(),
        P(),
        P(),
        P(),
        P(),
        P(),
        P(None, "rep", "shard", None),
        P(None, ("rep", "shard"), None, None),
    )
    out_specs = (
        P(None, "rep", "shard", None),
        P(None, ("rep", "shard"), None, None),
        P(None, "rep", "shard", None),
        P(None, ("rep", "shard"), None, None),
        P("shard", None),
        P(None, "shard", None),
        P("shard", None),
        P(),
        P(),
        P(),
        P(),
        P(),
        P(),
        P(),
        P(),
        P(),
    )
    return jax.shard_map(
        on_device, mesh=mesh, in_specs=in_specs, out_specs=out_specs, check_vma=False
    )
```

profile of v0, /device:TPU:0, one launch (start us, length us, event | category | flops | bytes accessed | tf_op | source)
XLA Modules:
  0.0 958.6 jit_solution(8579557248888360181)
XLA Ops:
  20.0 21.7 %all_gather.15 = bf16[800,400]{1,0:T(8,128)(2,1)S(1)} all-gather(bf16[200,400]{1,0:T(8,128)(2,1)S(1)} %convert_element_type.56), channel_id=1, replica_groups=mesh['rep'=8,'shard'=4] {'shard'}, dimensions={0}, use_global_device_ids=true | all-gather | bytes 800000 | tf_op jit(solution)/shard_map/all_gather | solution.py:101
  41.7 11.6 %fusion.17 = bf16[8,1024,800]{1,2,0:T(8,128)(2,1)} fusion(f32[800]{0:T(1024)S(1)} %copy-done.37, f32[800]{0:T(1024)S(1)} %copy-done.30, f32[8,1024]{1,0:T(8,128)S(1)} %add_rsqrt_fusion.2, f32[8,1024]{1,0:T(8,128)S(1)} %broadcast_multiply_fusion.8, bf16[8,512,800]{1,2,0:T(8,128)(2,1)S(1)} %bitcast.106, bf16[8,512,800]{1,2,0:T(8,128)(2,1)S(1)} %bitcast.114), kind=kLoop, calls=%fused_computation.27 | loop fusion | flops 85196800 | bytes 26286336 | tf_op jit(solution)/shard_map/convert_element_type | solution.py:107
  53.3 14.4 %add_reduce_fusion.1 = (f32[8,1024]{1,0:T(8,128)S(1)}, f32[8,1024,400]{1,2,0:T(8,128)S(1)}) fusion(f32[400]{0:T(512)S(1)} %copy-done.26, bf16[8,1024,800]{1,2,0:T(8,128)(2,1)} %fusion.17, bf16[800,400]{1,0:T(8,128)(2,1)S(1)} %all_gather.15), kind=kOutput, calls=%fused_computation.66 | convolution fusion | flops 5249425408 | bytes 26888768 | tf_op jit(solution)/shard_map/mrd,de->mre/dot_general | solution.py:109
  91.1 43.4 %all-reduce.17.cloned.1.call-done = bf16[8,32,400]{1,2,0:T(8,128)(2,1)} async-done(((bf16[8,32,400]{1,2,0:T(8,128)(2,1)}), bf16[8,32,400]{1,2,0:T(8,128)(2,1)}) %all-reduce.17.cloned.1.call-update) | async-done | bytes 204816 | tf_op jit(solution)/shard_map/psum | solution.py:18
  138.9 17.7 %all-gather = bf16[4,100,800]{2,1,0:T(8,128)(2,1)S(1)} all-gather(bf16[1,100,800]{2,1,0:T(8,128)(2,1)S(1)} %convert_bitcast_fusion), channel_id=1, replica_groups=mesh['rep'=8,'shard'=4] {'shard'}, dimensions={0}, use_global_device_ids=true | all-gather | bytes 800000 | tf_op jit(solution)/shard_map/all_gather | solution.py:103
  157.8 28.1 %all_gather.17 = bf16[3,400,400]{2,0,1:T(4,128)(2,1)S(1)} all-gather(bf16[3,100,400]{2,0,1:T(4,128)(2,1)S(1)} %copy.125), channel_id=1, replica_groups=mesh['rep'=8,'shard'=4] {'shard'}, dimensions={1}, use_global_device_ids=true | all-gather | bytes 1200000 | tf_op jit(solution)/shard_map/all_gather | solution.py:102
  203.8 47.6 %gather_fusion.1 = bf16[4096,400]{1,0:T(8,128)(2,1)} fusion(bf16[8,256,400]{2,1,0:T(8,128)(2,1)S(1)} %copy.119, s32[4096]{0:T(1024)S(1)} %bitcast.97), kind=kCustom, calls=%fused_computation.1 | custom fusion | bytes 6586368 | tf_op jit(solution)/shard_map/vmap()/gather | solution.py:71
  257.6 47.6 %gather_fusion = bf16[4096,400]{1,0:T(8,128)(2,1)} fusion(bf16[8,256,400]{2,1,0:T(8,128)(2,1)S(1)} %copy.119, s32[4096]{0:T(1024)S(1)} %bitcast.96), kind=kCustom, calls=%fused_computation | custom fusion | bytes 6586368 | tf_op jit(solution)/shard_map/vmap()/gather | solution.py:71
  311.6 9.7 %fusion.30 = (bf16[8,512,400]{1,2,0:T(8,128)(2,1)}, bf16[8,512,400]{1,2,0:T(8,128)(2,1)}) fusion(bf16[8,512,400]{1,2,0:T(8,128)(2,1)} %copy.121, bf16[8,512,400]{1,2,0:T(8,128)(2,1)} %get-tuple-element.152, pred[8,512]{1,0:T(8,128)(4,1)S(1)} %get-tuple-element.162, bf16[8,512,400]{1,2,0:T(8,128)(2,1)} %copy.124, pred[8,512]{1,0:T(8,128)(4,1)S(1)} %get-tuple-element.161), kind=kLoop, calls=%fused_computation.81 | loop fusion | flops 3276800 | bytes 16392192 | tf_op jit(solution)/shard_map/jit(_where)/select_n | solution.py:152
  321.4 13.6 %fusion.29 = bf16[8,1024,1200]{1,2,0:T(8,128)(2,1)} fusion(bf16[8,512,400]{1,2,0:T(8,128)(2,1)} %copy-done.5, bf16[8,32,400]{1,2,0:T(8,128)(2,1)} %copy.117, bf16[8,512,400]{1,2,0:T(8,128)(2,1)} %get-tuple-element.157, bf16[8,512,400]{1,2,0:T(8,128)(2,1)} %get-tuple-element.156, bf16[8,512,400]{1,2,0:T(8,128)(2,1)S(1)} %copy-done.4, ...), kind=kLoop, calls=%fused_computation.40 | loop fusion | flops 186777600 | bytes 36249600 | tf_op jit(solution)/shard_map/concatenate | solution.py:154
  335.0 15.7 %add_reduce_fusion = (f32[8,1024]{1,0:T(8,128)S(1)}, f32[8,1024,400]{1,2,0:T(8,128)S(1)}) fusion(f32[400]{0:T(512)S(1)} %copy-done.36, bf16[8,1024,1200]{1,2,0:T(8,128)(2,1)} %fusion.29, bf16[1200,400,1]{1,0,2:T(8,128)(2,1)} %bitcast.132), kind=kOutput, calls=%fused_computation.65 | convolution fusion | flops 7870865408 | bytes 33762368 | tf_op jit(solution)/shard_map/mrk,ke->mre/dot_general | solution.py:157
  352.7 18.3 %multiply_reduce_fusion.1 = (f32[400]{0:T(512)}, f32[8,1024]{1,0:T(8,128)S(1)}, f32[8,1024]{1,0:T(8,128)S(1)}, f32[400]{0:T(512)}, f32[8,1024,400]{1,2,0:T(8,128)}) fusion(f32[8,1024]{1,0:T(8,128)S(1)} %add_rsqrt_fusion, f32[8,1024]{1,0:T(8,128)S(1)} %broadcast_multiply_fusion.4, f32[8,1024,400]{1,2,0:T(8,128)S(1)} %get-tuple-element.168, ...), kind=kOutput, calls=%fused_computation.46 | convolution fusion | flops 5334612992 | bytes 40100672 | tf_op jit(solution)/shard_map/mrd,id->mri/dot_general | solution.py:174
  371.1 13.8 %fusion.61 = (f32[400]{0:T(512)}, bf16[8,1024,400]{1,2,0:T(8,128)(2,1)}, bf16[8,1024,400]{1,2,0:T(8,128)(2,1)}) fusion(f32[8,1024]{1,0:T(8,128)S(1)} %get-tuple-element.171, f32[8,1024]{1,0:T(8,128)S(1)} %broadcast_multiply_fusion.4, f32[8,1024,400]{1,2,0:T(8,128)S(1)} %get-tuple-element.168, f32[400]{0:T(512)S(1)} %copy-done.36, ...), kind=kLoop, calls=%fused_computation.150 | loop fusion | flops 55705200 | bytes 39459072 | tf_op jit(solution)/shard_map/reduce_sum | solution.py:43
  384.9 20.0 %fusion.36 = f32[1200,400,1]{1,0,2:T(8,128)} fusion(bf16[8,1024,1200]{1,2,0:T(8,128)(2,1)} %fusion.29, bf16[8,1024,400]{1,2,0:T(8,128)(2,1)} %get-tuple-element.127), kind=kOutput, calls=%fused_computation.87 | convolution fusion | flops 7864320000 | bytes 28134400 | tf_op jit(solution)/shard_map/mrk,mre->ke/dot_general | solution.py:183
  404.9 16.9 %fusion.38 = f32[8,1024,1200]{1,2,0:T(8,128)} fusion(bf16[1200,400,1]{1,0,2:T(8,128)(2,1)S(1)} %bitcast.133, bf16[8,1024,400]{1,2,0:T(8,128)(2,1)S(1)} %copy-done.6), kind=kOutput, calls=%fused_computation.89 | convolution fusion | flops 7864320000 | bytes 46835200 | tf_op jit(solution)/shard_map/mre,ke->mrk/dot_general | solution.py:186
  421.9 13.6 %convolution_bitcast_fusion = f32[400,800]{1,0:T(8,128)S(1)} fusion(bf16[8,1024,400]{1,2,0:T(8,128)(2,1)} %get-tuple-element.147, bf16[8,512,800]{1,2,0:T(8,128)(2,1)} %bitcast.126, bf16[8,512,800]{1,2,0:T(8,128)(2,1)} %bitcast.129), kind=kOutput, calls=%fused_computation.98 | convolution fusion | flops 5269094400 | bytes 20940800 | tf_op jit(solution)/shard_map/mri,mrd->id/dot_general | solution.py:173
  435.5 30.3 %fusion = f32[112,800]{1,0:T(8,128)S(1)} fusion(f32[400,800]{1,0:T(8,128)S(1)} %convolution_bitcast_fusion), kind=kCustom, calls=%all-reduce-scatter | all-reduce-scatter fusion | flops 358401 | bytes 1638912
  467.9 16.2 %fusion.26 = bf16[8,1024,800]{1,2,0:T(8,128)(2,1)} fusion(f32[800]{0:T(1024)S(1)} %copy-done.48, bf16[8,1024,400]{1,2,0:T(8,128)(2,1)} %get-tuple-element.147, bf16[400,800,1]{1,0,2:T(8,128)(2,1)S(1)} %copy-done.12, bf16[8,512,800]{1,2,0:T(8,128)(2,1)} %bitcast.101, bf16[8,512,800]{1,2,0:T(8,128)(2,1)} %bitcast.111), kind=kOutput, calls=%fused_computation.36 | convolution fusion | flops 5288755200 | bytes 33411200 | tf_op jit(solution)/shard_map/mri,id->mrd/dot_general | solution.py:162
  484.1 30.9 %slice_select_fusion.2 = (f32[8,512,400]{1,2,0:T(8,128)}, f32[8,512,400]{1,2,0:T(8,128)}, f32[8,512,400]{1,2,0:T(8,128)}, f32[8,512,400]{1,2,0:T(8,128)}, f32[8,...) fusion(f32[8,1024,1200]{1,2,0:T(8,128)} %fusion.38, ...), kind=kLoop, calls=%fused_computation.74 | loop fusion | flops 8192000 | bytes 91762688 | tf_op jit(solution)/shard_map/jit(_where)/select_n | solution.py:226
  532.0 31.4 %scatter_custom_fusion.1 = f32[2048,400]{1,0:T(8,128)} fusion(s32[4096]{0:T(1024)} %bitcast.135, f32[4096,400]{1,0:T(8,128)} %bitcast.124, f32[]{:T(128)} %constant.48.clone.1), kind=kCustom, calls=%fused_computation.91 | custom fusion | flops 1638400 | bytes 3277312
  563.4 31.7 %scatter_custom_fusion = f32[2048,400]{1,0:T(8,128)} fusion(s32[4096]{0:T(1024)} %bitcast.134, f32[4096,400]{1,0:T(8,128)} %bitcast.123, f32[]{:T(128)} %constant.48.clone.1), kind=kCustom, calls=%fused_computation.93 | custom fusion | flops 1638400 | bytes 3277312
  621.1 10.7 %slice_bitcast_fusion.2 = (bf16[8,1,512,800]{2,3,1,0:T(8,128)(2,1)}, bf16[8,1,512,800]{2,3,1,0:T(8,128)(2,1)}) fusion(bf16[8,1024,800]{1,2,0:T(8,128)(2,1)} %fusion.26), kind=kLoop, calls=%fused_computation.71 | loop fusion | bytes 26214400
  631.9 11.0 %pad_add_fusion.1 = f32[8,512,400]{1,2,0:T(8,128)} fusion(f32[8,512,400]{1,2,0:T(8,128)} %get-tuple-element.136, f32[8,512,400]{1,2,0:T(8,128)} %get-tuple-element.140, f32[8,512,400]{1,2,0:T(8,128)} %get-tuple-element.139), kind=kLoop, calls=%fused_computation.68 | loop fusion | flops 3276800 | bytes 26214400 | tf_op jit(solution)/shard_map/add | solution.py:214
  652.4 92.5 %all-reduce.19.cloned.1.call-done = f32[8,256,400]{1,2,0:T(8,128)} async-done(((f32[8,256,400]{1,2,0:T(8,128)}), f32[8,256,400]{1,2,0:T(8,128)}) %all-reduce.19.cloned.1.call-update) | async-done | bytes 3276816 | tf_op jit(solution)/shard_map/psum | solution.py:235
  747.7 21.0 %multiply_reduce_fusion.2 = (f32[400]{0:T(512)S(1)}, f32[8,1024]{1,0:T(8,128)S(1)}, f32[8,1024]{1,0:T(8,128)S(1)}, f32[400]{0:T(512)S(1)}, f32[8,1024,400]{1,2,0:T(8,128)}) fusion(f32[8,1024]{1,0:T(8,128)S(1)} %copy-done.17, f32[8,1024]{1,0:T(8,128)S(1)} %copy-done.10, f32[8,1024,400]{1,2,0:T(8,128)} %copy-done, f32[400]{0:T(512)S(1)} %copy-done.27, ...), kind=kLoop, calls=%fused_computation.47 | loop fusion | flops 72072416 | bytes 39460672 | tf_op jit(solution)/shard_map/reduce_sum | solution.py:43
  768.7 10.1 %fusion.62 = (f32[400]{0:T(512)S(1)}, bf16[8,1024,400]{1,2,0:T(8,128)(2,1)}) fusion(f32[8,1024]{1,0:T(8,128)S(1)} %broadcast_multiply_fusion, f32[8,1024]{1,0:T(8,128)S(1)} %copy-done.10, f32[8,1024,400]{1,2,0:T(8,128)S(1)} %bitcast.99, f32[400]{0:T(512)S(1)} %copy-done.27, f32[8,1024]{1,0:T(8,128)S(1)} %broadcast_multiply_fusion.1, ...), kind=kLoop, calls=%fused_computation.151 | loop fusion | flops 32767600 | bytes 32903872 | tf_op jit(solution)/shard_map/reduce_sum | solution.py:43
  778.9 25.9 %fusion.24 = (f32[800]{0:T(1024)S(1)}, f32[8,1024]{1,0:T(8,128)S(1)}, f32[8,1024]{1,0:T(8,128)S(1)}, f32[800]{0:T(1024)S(1)}, f32[8,1024,800]{1,2,0:T(8,128)}) fusion(f32[8,1024]{1,0:T(8,128)S(1)} %copy-done.21, f32[8,1024]{1,0:T(8,128)S(1)} %copy-done.15, bf16[8,512,800]{1,2,0:T(8,128)(2,1)S(1)} %bitcast.109, bf16[8,512,800]{1,2,0:T(8,128)(2,1)S(1)} %bitcast.117, ...), kind=kOutput, calls=%fused_computation.34 | convolution fusion | flops 5393594368 | bytes 46659072 | tf_op jit(solution)/shard_map/mre,de->mrd/dot_general | solution.py:263
  804.9 10.3 %fusion.44 = f32[800,400]{1,0:T(8,128)} fusion(bf16[8,1024,800]{1,2,0:T(8,128)(2,1)S(1)} %bitcast.122, bf16[8,1024,400]{1,2,0:T(8,128)(2,1)} %get-tuple-element.129), kind=kOutput, calls=%fused_computation.97 | convolution fusion | flops 5242880000 | bytes 20940800 | tf_op jit(solution)/shard_map/mrd,mre->de/dot_general | solution.py:260
  815.3 28.3 %convert_reduce_fusion.1 = (f32[800]{0:T(1024)S(1)}, f32[8,1024,800]{1,2,0:T(8,128)}) fusion(bf16[8,512,800]{1,2,0:T(8,128)(2,1)} %bitcast.127, bf16[8,512,800]{1,2,0:T(8,128)(2,1)} %bitcast.130, f32[8,1024]{1,0:T(8,128)S(1)} %broadcast_multiply_fusion.6, f32[8,1024]{1,0:T(8,128)S(1)} %copy-done.15, bf16[8,512,800]{1,2,0:T(8,128)(2,1)} %bitcast.102, ...), kind=kLoop, calls=%fused_computation.12 | loop fusion | flops 111410400 | bytes 78780672 | tf_op jit(solution)/shard_map/reduce_sum | solution.py:43
  847.5 36.2 %reduce-scatter.5.cloned.1.call-done = f32[200,400]{1,0:T(8,128)} async-done(((f32[800,400]{1,0:T(8,128)}), f32[200,400]{1,0:T(8,128)}) %reduce-scatter.5.cloned.1.call-update) | async-done | bytes 320016 | tf_op jit(solution)/shard_map/reduce_scatter | solution.py:275
  883.8 17.0 %slice_bitcast_fusion = (f32[8,1,512,800]{2,3,1,0:T(8,128)}, f32[8,1,512,800]{2,3,1,0:T(8,128)}) fusion(f32[8,1024,800]{1,2,0:T(8,128)} %get-tuple-element.149), kind=kLoop, calls=%fused_computation.41 | loop fusion | bytes 52428800
  900.8 40.0 %all-reduce.10 = (f32[800]{0:T(1024)}, f32[800]{0:T(1024)}, f32[400]{0:T(512)}, f32[400]{0:T(512)}, f32[400]{0:T(512)}, /*index=5*/f32[400]{0:T(512)}, f32[400]{0:T(512)}, f32[400]{0:T(512)}, f32[800]{0:T(1024)}) all-reduce(f32[800]{0:T(1024)S(1)} %get-tuple-element.96, ...), channel_id=1, replica_groups=mesh['rep'=8,'shard'=4] {'rep','shard'}, use_global_device_ids=true, to_apply=%region_26.27 | all-reduce | flops 4800 | bytes 38400 | tf_op jit(solution)/shard_map/psum | solution.py:270
  (214 shorter events, 144.7 us)
Async XLA Ops:
  7.2 127.3 %all-reduce.17.cloned.1.call-start = ((), (), s32[]{:S(2)}) async-start(), calls=%async_computation.1 | async-start | bytes 1638400 | tf_op jit(solution)/shard_map/psum | solution.py:18
  7.3 34.4 %copy-start.30 = (f32[800]{0:T(1024)S(1)}, f32[800]{0:T(1024)}, u32[]{:S(2)}) copy-start(f32[800]{0:T(1024)} %param.25) | copy-start | bytes 9604
  7.3 34.3 %copy-start.37 = (f32[800]{0:T(1024)S(1)}, f32[800]{0:T(1024)}, u32[]{:S(2)}) copy-start(f32[800]{0:T(1024)} %param.26) | copy-start | bytes 9604
  74.6 62.2 %copy-start.39 = (s32[8,1,2]{0,2,1:T(2,128)S(1)}, s32[8,1,2]{0,2,1:T(2,128)}, u32[]{:S(2)}) copy-start(s32[8,1,2]{0,2,1:T(2,128)} %param.21) | copy-start | bytes 196
  74.7 62.3 %copy-start.45 = (s32[8,1,2]{0,2,1:T(2,128)S(1)}, s32[8,1,2]{0,2,1:T(2,128)}, u32[]{:S(2)}) copy-start(s32[8,1,2]{0,2,1:T(2,128)} %param.20) | copy-start | bytes 196
  74.7 62.4 %copy-start.47 = (s32[2]{0:T(128)S(1)}, s32[2]{0:T(128)}, u32[]{:S(2)}) copy-start(s32[2]{0:T(128)} %constant.84) | copy-start | bytes 28
  74.7 62.5 %copy-start.46 = (s32[2]{0:T(128)S(1)}, s32[2]{0:T(128)}, u32[]{:S(2)}) copy-start(s32[2]{0:T(128)} %constant.87) | copy-start | bytes 28
  74.7 63.8 %copy-start.13 = (f32[3,100,400]{1,2,0:T(8,128)S(1)}, f32[3,100,400]{1,2,0:T(8,128)}, u32[]{:S(2)}) copy-start(f32[3,100,400]{1,2,0:T(8,128)} %param.23) | copy-start | bytes 1440004
  75.3 63.6 %copy-start.19 = (f32[100,800]{1,0:T(8,128)S(1)}, f32[100,800]{1,0:T(8,128)}, u32[]{:S(2)}) copy-start(f32[100,800]{1,0:T(8,128)} %param.24) | copy-start | bytes 960004
  75.3 111.9 %copy-start.44 = (u32[32]{0:T(128)S(1)}, u32[32]{0:T(128)}, u32[]{:S(2)}) copy-start(u32[32]{0:T(128)} %constant.127) | copy-start | bytes 388
  87.4 114.1 %all-gather.3.cloned.1.call-start = ((), (), s32[]{:S(2)}) async-start(), calls=%async_computation.2 | async-start | bytes 2359296 | tf_op jit(solution)/shard_map/all_gather | solution.py:118
  88.8 106.2 %collective-permute-start = (bf16[8,32,400]{2,1,0:T(8,128)(2,1)}, bf16[8,32,400]{2,1,0:T(8,128)(2,1)}, u32[]{:S(2)}, u32[]{:S(2)}) collective-permute-start(bf16[8,32,400]{2,1,0:T(8,128)(2,1)} %copy.116), channel_id=1, source_target_pairs={{0,1},{1,2},{2,3},{4,5},{5,6},{6,7},{8,9},{9,10},{10,11},{12,13},{... | collective-permute-start | bytes 614408 | tf_op jit(solution)/shard_map/ppermute | solution.py:13
  136.8 608.1 %all-reduce.19.cloned.1.call-start = ((), (), s32[]{:S(2)}) async-start(), calls=%async_computation.3 | async-start | bytes 6553600 | tf_op jit(solution)/shard_map/psum | solution.py:235
  195.0 116.6 %copy-start.22 = (pred[8,512]{1,0:T(8,128)(4,1)}, pred[8,512]{1,0:T(8,128)(4,1)S(1)}, u32[]{:S(2)}) copy-start(pred[8,512]{1,0:T(8,128)(4,1)S(1)} %get-tuple-element.161) | copy-start | bytes 12292
  195.0 116.6 %copy-start.24 = (pred[8,512]{1,0:T(8,128)(4,1)}, pred[8,512]{1,0:T(8,128)(4,1)S(1)}, u32[]{:S(2)}) copy-start(pred[8,512]{1,0:T(8,128)(4,1)S(1)} %get-tuple-element.162) | copy-start | bytes 12292
  421.9 46.1 %copy-start.12 = (bf16[400,800,1]{1,0,2:T(8,128)(2,1)S(1)}, bf16[400,800,1]{1,0,2:T(8,128)(2,1)}, u32[]{:S(2)}) copy-start(bf16[400,800,1]{1,0,2:T(8,128)(2,1)} %reshape.260) | copy-start | bytes 1920004
  421.9 46.1 %copy-start.48 = (f32[800]{0:T(1024)S(1)}, f32[800]{0:T(1024)}, u32[]{:S(2)}) copy-start(f32[800]{0:T(1024)} %param.33) | copy-start | bytes 9604
  465.8 185.1 %collective-permute-start.2 = (f32[36,800]{1,0:T(8,128)S(1)}, f32[36,800]{1,0:T(8,128)S(1)}, u32[]{:S(2)}, u32[]{:S(2)}) collective-permute-start(f32[36,800]{1,0:T(8,128)S(1)} %slice.111), channel_id=1, source_target_pairs={{0,1},{1,2},{2,3},{4,5},{5,6},{6,7},{8,9},{9,10},{10,11},{12,13},{... | collective-permute-start | bytes 345608
  606.8 238.7 %all-reduce.21.cloned.1.call-start = ((), (), s32[]{:S(2)}) async-start(), calls=%async_computation.5 | async-start | bytes 4915200
  619.8 32.3 %collective-permute-start.1 = (bf16[8,32,400]{2,1,0:T(8,128)(2,1)S(1)}, bf16[8,32,400]{2,1,0:T(8,128)(2,1)S(1)}, u32[]{:S(2)}, u32[]{:S(2)}) collective-permute-start(bf16[8,32,400]{2,1,0:T(8,128)(2,1)S(1)} %copy.129), channel_id=1, source_target_pairs={{1,0},{2,1},{3,2},{5,4},{6,5},{7,6},{9,8},{10,9},{11,10},{13,12},{... | collective-permute-start | bytes 614408 | tf_op jit(solution)/shard_map/ppermute | solution.py:13
  631.8 251.9 %reduce-scatter.5.cloned.1.call-start = ((), (), s32[]{:S(2)}) async-start(), calls=%async_computation.4 | async-start | bytes 2048000 | tf_op jit(solution)/shard_map/reduce_scatter | solution.py:275
  642.8 104.7 %copy-start.10 = (f32[8,1024]{1,0:T(8,128)S(1)}, f32[8,1024]{1,0:T(8,128)}, u32[]{:S(2)}) copy-start(f32[8,1024]{1,0:T(8,128)} %copy-done.9) | copy-start | bytes 98308
  642.8 104.7 %copy-start.17 = (f32[8,1024]{1,0:T(8,128)S(1)}, f32[8,1024]{1,0:T(8,128)}, u32[]{:S(2)}) copy-start(f32[8,1024]{1,0:T(8,128)} %copy-done.16) | copy-start | bytes 98308
  642.8 104.7 %copy-start.27 = (f32[400]{0:T(512)S(1)}, f32[400]{0:T(512)}, u32[]{:S(2)}) copy-start(f32[400]{0:T(512)} %param.27) | copy-start | bytes 4804
  642.8 104.8 %copy-start.29 = (f32[400]{0:T(512)S(1)}, f32[400]{0:T(512)}, u32[]{:S(2)}) copy-start(f32[400]{0:T(512)} %param.28) | copy-start | bytes 4804
  642.8 104.8 %copy-start.34 = (f32[400]{0:T(512)S(1)}, f32[400]{0:T(512)}, u32[]{:S(2)}) copy-start(f32[400]{0:T(512)} %param.29) | copy-start | bytes 4804
  745.0 33.9 %slice-start.6 = ((s8[6553600]{0:T(1024)(128)(4,1)}), s8[4194304]{0:T(1024)(128)(4,1)S(1)}, s32[]{:S(2)}) async-start(s8[6553600]{0:T(1024)(128)(4,1)} %bitcast.107), calls=%async_computation.13 | async-start | bytes 8388608
  745.0 33.9 %slice-start.8 = ((s8[6553600]{0:T(1024)(128)(4,1)}), s8[4194304]{0:T(1024)(128)(4,1)S(1)}, s32[]{:S(2)}) async-start(s8[6553600]{0:T(1024)(128)(4,1)} %bitcast.115), calls=%async_computation.15 | async-start | bytes 8388608
  747.6 31.2 %slice-start.7 = ((s8[6553600]{0:T(1024)(128)(4,1)}), s8[2359296]{0:T(1024)(128)(4,1)S(1)}, s32[]{:S(2)}) async-start(s8[6553600]{0:T(1024)(128)(4,1)} %bitcast.107), calls=%async_computation.14 | async-start | bytes 4718592
  747.6 31.2 %slice-start.9 = ((s8[6553600]{0:T(1024)(128)(4,1)}), s8[2359296]{0:T(1024)(128)(4,1)S(1)}, s32[]{:S(2)}) async-start(s8[6553600]{0:T(1024)(128)(4,1)} %bitcast.115), calls=%async_computation.16 | async-start | bytes 4718592
  768.7 36.2 %slice-start.10 = ((s8[13107200]{0:T(1024)(128)(4,1)}), s8[524288]{0:T(1024)(128)(4,1)S(1)}, s32[]{:S(2)}) async-start(s8[13107200]{0:T(1024)(128)(4,1)} %bitcast.121), calls=%async_computation.17 | async-start | bytes 1048576
  815.2 130.4 %all-reduce.23.cloned.1.call-start = ((), (), s32[]{:S(2)}) async-start(), calls=%async_computation.6 | async-start | bytes 2842624 | tf_op jit(solution)/shard_map/psum | solution.py:279
  (40 other events, 537.4 us)
Sparse Core Ops, SparseCore 0:
  87.5 46.8 all-reduce.16
  136.9 27.0 all-gather.2
  606.9 138.0 all-reduce.18
  747.3 98.1 all-reduce.20
  848.4 35.3 reduce-scatter.4
  887.7 57.8 all-reduce.22
where the time goes:
time: 968 us; the launch traced here: 959 us
  other arithmetic  262 us (27%)
  local copies, waits for them, and re-layouts  205 us (21%)
  waiting for transfers between devices  179 us (18%)
  matrix products  151 us (16%)
  blocking collectives  138 us (14%)
  between operations  16.9 us (2%)
    gather x4, local copies, waits for them, and re-layouts, pick_rows(): block[where_from]  108 us
    psum x1, waiting for transfers between devices, on_device(): lax.psum((tail_part, part_bias_conv, part_gain_three, part_shift_three, p...  92.5 us
    reduce_sum x4, other arithmetic, row_total(): return jnp.sum(values, axis=(0, 1))  73.2 us
    unnamed x12, other arithmetic  63.2 us
    unnamed x142, local copies, waits for them, and re-layouts  51.5 us
    psum x1, waiting for transfers between devices, from_root(): return lax.psum(kept, axis)  43.4 us
    psum x1, blocking collectives, on_device(): lax.psum((part_gain_one, part_shift_one, part_bias_in, part_gain_two, par...  40 us
    reduce_scatter x1, waiting for transfers between devices, on_device(): lax.psum_scatter(full_w_in, 'shard', scatter_dimension=0, tiled=True)  36.2 us
  transfers between devices with their start and end apart: 9, of which 5 were waited for; matrix products, arithmetic and copies ran while one was open for 33% of the time, Pallas kernels for 0%

commit v1 on v0

--- a/solution.py
+++ b/solution.py
@@ -15,7 +15,7 @@
 
 def from_root(value, axis, source):
     kept = jnp.where(lax.axis_index(axis) == source, value, 0).astype(value.dtype)
-    return lax.psum(kept, axis)
+    return jnp.sum(lax.all_gather(kept, axis), axis=0)
 
 
 def norm_forward(values, gain, shift_by):

time: 968 us -> 1080 us (1.12)
  local copies, waits for them, and re-layouts: 205 us -> 345 us
  waiting for transfers between devices: 179 us -> 134 us
  blocking collectives: 138 us -> 149 us
    gather x4, local copies, waits for them, and re-layouts: 108 us -> 252 us  [pick_rows(): block[where_from]]
    psum x1 -> x0, waiting for transfers between devices: 43.4 us -> none  [from_root(): return lax.psum(kept, axis)]
    all_gather x0 -> x1, blocking collectives: none -> 24.5 us  [from_root(): return jnp.sum(lax.all_gather(kept, axis), axis=0)]
    unnamed x142 -> x144, local copies, waits for them, and re-layouts: 51.5 us -> 51.5 us
  transfers between devices with their start and end apart: 9 -> 8, of which waited for: 5 -> 4; matrix products, arithmetic and copies ran while one was open for 33% -> 30% of each run, Pallas kernels for 0% -> 0%
where the time goes in v1:
time: 1080 us; the launch traced here: 1060 us
  local copies, waits for them, and re-layouts  345 us (32%)
  other arithmetic  262 us (24%)
  matrix products  151 us (14%)
  blocking collectives  149 us (14%)
  waiting for transfers between devices  134 us (12%)
  between operations  16.5 us (2%)
    gather x4, local copies, waits for them, and re-layouts, pick_rows(): block[where_from]  252 us
    psum x1, waiting for transfers between devices, on_device(): lax.psum((tail_part, part_bias_conv, part_gain_three, part_shift_three, p...  91 us
    reduce_sum x4, other arithmetic, row_total(): return jnp.sum(values, axis=(0, 1))  73.2 us
    unnamed x12, other arithmetic  63.2 us
    unnamed x144, local copies, waits for them, and re-layouts  51.5 us
    psum x1, blocking collectives, on_device(): lax.psum((part_gain_one, part_shift_one, part_bias_in, part_gain_two, par...  39.9 us
    reduce_scatter x1, waiting for transfers between devices, on_device(): lax.psum_scatter(full_w_in, 'shard', scatter_dimension=0, tiled=True)  36.2 us
    select_n x1, other arithmetic, on_device(): far_piece = jnp.where(keep_near, 0.0, cont_piece)  30.9 us
  transfers between devices with their start and end apart: 8, of which 4 were waited for; matrix products, arithmetic and copies ran while one was open for 30% of the time, Pallas kernels for 0%

profile of v1, /device:TPU:0, one launch (start us, length us, event | category | flops | bytes accessed | tf_op | source)
XLA Modules:
  0.0 1064.0 jit_solution(1002727523576614458)
XLA Ops:
  20.0 21.7 %all_gather.21 = bf16[800,400]{1,0:T(8,128)(2,1)S(1)} all-gather(bf16[200,400]{1,0:T(8,128)(2,1)S(1)} %convert_element_type.58), channel_id=1, replica_groups=mesh['rep'=8,'shard'=4] {'shard'}, dimensions={0}, use_global_device_ids=true | all-gather | bytes 800000 | tf_op jit(solution)/shard_map/all_gather | solution.py:101
  41.7 11.6 %fusion.17 = bf16[8,1024,800]{1,2,0:T(8,128)(2,1)} fusion(f32[800]{0:T(1024)S(1)} %copy-done.38, f32[800]{0:T(1024)S(1)} %copy-done.31, f32[8,1024]{1,0:T(8,128)S(1)} %add_rsqrt_fusion.2, f32[8,1024]{1,0:T(8,128)S(1)} %broadcast_multiply_fusion.8, bf16[8,512,800]{1,2,0:T(8,128)(2,1)S(1)} %bitcast.107, bf16[8,512,800]{1,2,0:T(8,128)(2,1)S(1)} %bitcast.115), kind=kLoop, calls=%fused_computation.27 | loop fusion | flops 85196800 | bytes 26286336 | tf_op jit(solution)/shard_map/convert_element_type | solution.py:107
  53.3 14.4 %add_reduce_fusion.1 = (f32[8,1024]{1,0:T(8,128)S(1)}, f32[8,1024,400]{1,2,0:T(8,128)S(1)}) fusion(f32[400]{0:T(512)S(1)} %copy-done.27, bf16[8,1024,800]{1,2,0:T(8,128)(2,1)} %fusion.17, bf16[800,400]{1,0:T(8,128)(2,1)S(1)} %all_gather.21), kind=kOutput, calls=%fused_computation.66 | convolution fusion | flops 5249425408 | bytes 26888768 | tf_op jit(solution)/shard_map/mrd,de->mre/dot_general | solution.py:109
  90.1 24.5 %all-gather = bf16[32,32,400]{2,1,0:T(8,128)(2,1)S(1)} all-gather(bf16[8,32,400]{2,1,0:T(8,128)(2,1)S(1)} %copy.112), channel_id=2, replica_groups=mesh['rep'=8,'shard'=4] {'shard'}, dimensions={0}, use_global_device_ids=true | all-gather | bytes 1024000 | tf_op jit(solution)/shard_map/all_gather | solution.py:18
  117.7 18.0 %all-gather.1 = bf16[4,100,800]{2,1,0:T(8,128)(2,1)S(1)} all-gather(bf16[1,100,800]{2,1,0:T(8,128)(2,1)S(1)} %convert_bitcast_fusion), channel_id=1, replica_groups=mesh['rep'=8,'shard'=4] {'shard'}, dimensions={0}, use_global_device_ids=true | all-gather | bytes 800000 | tf_op jit(solution)/shard_map/all_gather | solution.py:103
  136.8 24.9 %all_gather.25 = bf16[3,400,400]{2,0,1:T(4,128)(2,1)S(1)} all-gather(bf16[3,100,400]{2,0,1:T(4,128)(2,1)S(1)} %copy.119), channel_id=1, replica_groups=mesh['rep'=8,'shard'=4] {'shard'}, dimensions={1}, use_global_device_ids=true | all-gather | bytes 1200000 | tf_op jit(solution)/shard_map/all_gather | solution.py:102
  177.3 191.6 %gather_fusion.1 = bf16[4096,400]{1,0:T(8,128)(2,1)} fusion(bf16[8,256,400]{2,1,0:T(8,128)(2,1)} %all-gather.4.cloned.1.call-done, s32[4096]{0:T(1024)S(1)} %bitcast.98), kind=kCustom, calls=%fused_computation.1 | custom fusion | bytes 6586368 | tf_op jit(solution)/shard_map/vmap()/gather | solution.py:71
  375.3 47.6 %gather_fusion = bf16[4096,400]{1,0:T(8,128)(2,1)} fusion(bf16[8,256,400]{2,1,0:T(8,128)(2,1)S(1)} %copy-done, s32[4096]{0:T(1024)S(1)} %bitcast.97), kind=kCustom, calls=%fused_computation | custom fusion | bytes 6586368 | tf_op jit(solution)/shard_map/vmap()/gather | solution.py:71
  429.3 9.8 fusion.30
  439.1 13.6 %fusion.29 = bf16[8,1024,1200]{1,2,0:T(8,128)(2,1)} fusion(bf16[8,512,400]{1,2,0:T(8,128)(2,1)} %copy-done.6, bf16[8,32,400]{1,2,0:T(8,128)(2,1)} %copy.111, bf16[8,512,400]{1,2,0:T(8,128)(2,1)} %get-tuple-element.157, bf16[8,512,400]{1,2,0:T(8,128)(2,1)} %get-tuple-element.156, bf16[8,512,400]{1,2,0:T(8,128)(2,1)S(1)} %copy-done.5, ...), kind=kLoop, calls=%fused_computation.40 | loop fusion | flops 186777600 | bytes 36249600 | tf_op jit(solution)/shard_map/concatenate | solution.py:154
  452.7 15.7 %add_reduce_fusion = (f32[8,1024]{1,0:T(8,128)S(1)}, f32[8,1024,400]{1,2,0:T(8,128)S(1)}) fusion(f32[400]{0:T(512)S(1)} %copy-done.37, bf16[8,1024,1200]{1,2,0:T(8,128)(2,1)} %fusion.29, bf16[1200,400,1]{1,0,2:T(8,128)(2,1)} %bitcast.134), kind=kOutput, calls=%fused_computation.65 | convolution fusion | flops 7870865408 | bytes 33762368 | tf_op jit(solution)/shard_map/mrk,ke->mre/dot_general | solution.py:157
  470.5 18.3 %multiply_reduce_fusion.1 = (f32[400]{0:T(512)}, f32[8,1024]{1,0:T(8,128)S(1)}, f32[8,1024]{1,0:T(8,128)S(1)}, f32[400]{0:T(512)}, f32[8,1024,400]{1,2,0:T(8,128)}) fusion(f32[8,1024]{1,0:T(8,128)S(1)} %add_rsqrt_fusion, f32[8,1024]{1,0:T(8,128)S(1)} %broadcast_multiply_fusion.4, f32[8,1024,400]{1,2,0:T(8,128)S(1)} %get-tuple-element.168, ...), kind=kOutput, calls=%fused_computation.46 | convolution fusion | flops 5334612992 | bytes 40100672 | tf_op jit(solution)/shard_map/mrd,id->mri/dot_general | solution.py:174
  488.8 13.8 %fusion.61 = (f32[400]{0:T(512)}, bf16[8,1024,400]{1,2,0:T(8,128)(2,1)}, bf16[8,1024,400]{1,2,0:T(8,128)(2,1)}) fusion(f32[8,1024]{1,0:T(8,128)S(1)} %get-tuple-element.171, f32[8,1024]{1,0:T(8,128)S(1)} %broadcast_multiply_fusion.4, f32[8,1024,400]{1,2,0:T(8,128)S(1)} %get-tuple-element.168, f32[400]{0:T(512)S(1)} %copy-done.37, ...), kind=kLoop, calls=%fused_computation.150 | loop fusion | flops 55705200 | bytes 39459072 | tf_op jit(solution)/shard_map/reduce_sum | solution.py:43
  502.7 20.0 %fusion.36 = f32[1200,400,1]{1,0,2:T(8,128)} fusion(bf16[8,1024,1200]{1,2,0:T(8,128)(2,1)} %fusion.29, bf16[8,1024,400]{1,2,0:T(8,128)(2,1)} %get-tuple-element.127), kind=kOutput, calls=%fused_computation.87 | convolution fusion | flops 7864320000 | bytes 28134400 | tf_op jit(solution)/shard_map/mrk,mre->ke/dot_general | solution.py:183
  522.7 16.9 %fusion.38 = f32[8,1024,1200]{1,2,0:T(8,128)} fusion(bf16[1200,400,1]{1,0,2:T(8,128)(2,1)S(1)} %bitcast.135, bf16[8,1024,400]{1,2,0:T(8,128)(2,1)S(1)} %copy-done.7), kind=kOutput, calls=%fused_computation.89 | convolution fusion | flops 7864320000 | bytes 46835200 | tf_op jit(solution)/shard_map/mre,ke->mrk/dot_general | solution.py:186
  539.6 13.6 %convolution_bitcast_fusion = f32[400,800]{1,0:T(8,128)S(1)} fusion(bf16[8,1024,400]{1,2,0:T(8,128)(2,1)} %get-tuple-element.147, bf16[8,512,800]{1,2,0:T(8,128)(2,1)} %bitcast.127, bf16[8,512,800]{1,2,0:T(8,128)(2,1)} %bitcast.130), kind=kOutput, calls=%fused_computation.98 | convolution fusion | flops 5269094400 | bytes 20940800 | tf_op jit(solution)/shard_map/mri,mrd->id/dot_general | solution.py:173
  553.2 20.5 %fusion = f32[112,800]{1,0:T(8,128)S(1)} fusion(f32[400,800]{1,0:T(8,128)S(1)} %convolution_bitcast_fusion), kind=kCustom, calls=%all-reduce-scatter | all-reduce-scatter fusion | flops 358401 | bytes 1638912
  575.4 16.1 %fusion.26 = bf16[8,1024,800]{1,2,0:T(8,128)(2,1)} fusion(f32[800]{0:T(1024)S(1)} %copy-done.49, bf16[8,1024,400]{1,2,0:T(8,128)(2,1)} %get-tuple-element.147, bf16[400,800,1]{1,0,2:T(8,128)(2,1)S(1)} %copy-done.13, bf16[8,512,800]{1,2,0:T(8,128)(2,1)} %bitcast.102, bf16[8,512,800]{1,2,0:T(8,128)(2,1)} %bitcast.112), kind=kOutput, calls=%fused_computation.36 | convolution fusion | flops 5288755200 | bytes 33411200 | tf_op jit(solution)/shard_map/mri,id->mrd/dot_general | solution.py:162
  591.6 30.9 %slice_select_fusion.2 = (f32[8,512,400]{1,2,0:T(8,128)}, f32[8,512,400]{1,2,0:T(8,128)}, f32[8,512,400]{1,2,0:T(8,128)}, f32[8,512,400]{1,2,0:T(8,128)}, f32[8,...) fusion(f32[8,1024,1200]{1,2,0:T(8,128)} %fusion.38, ...), kind=kLoop, calls=%fused_computation.74 | loop fusion | flops 8192000 | bytes 91762688 | tf_op jit(solution)/shard_map/jit(_where)/select_n | solution.py:226
  639.5 31.4 %scatter_custom_fusion.1 = f32[2048,400]{1,0:T(8,128)} fusion(s32[4096]{0:T(1024)} %bitcast.137, f32[4096,400]{1,0:T(8,128)} %bitcast.125, f32[]{:T(128)} %constant.49.clone.1), kind=kCustom, calls=%fused_computation.91 | custom fusion | flops 1638400 | bytes 3277312
  670.9 31.7 %scatter_custom_fusion = f32[2048,400]{1,0:T(8,128)} fusion(s32[4096]{0:T(1024)} %bitcast.136, f32[4096,400]{1,0:T(8,128)} %bitcast.124, f32[]{:T(128)} %constant.49.clone.1), kind=kCustom, calls=%fused_computation.93 | custom fusion | flops 1638400 | bytes 3277312
  728.6 10.7 %slice_bitcast_fusion.2 = (bf16[8,1,512,800]{2,3,1,0:T(8,128)(2,1)}, bf16[8,1,512,800]{2,3,1,0:T(8,128)(2,1)}) fusion(bf16[8,1024,800]{1,2,0:T(8,128)(2,1)} %fusion.26), kind=kLoop, calls=%fused_computation.71 | loop fusion | bytes 26214400
  739.4 10.7 %pad_add_fusion.1 = f32[8,512,400]{1,2,0:T(8,128)} fusion(f32[8,512,400]{1,2,0:T(8,128)} %get-tuple-element.136, f32[8,512,400]{1,2,0:T(8,128)} %get-tuple-element.140, f32[8,512,400]{1,2,0:T(8,128)} %get-tuple-element.139), kind=kLoop, calls=%fused_computation.68 | loop fusion | flops 3276800 | bytes 26214400 | tf_op jit(solution)/shard_map/add | solution.py:214
  759.5 91.0 %all-reduce.16.cloned.1.call-done = f32[8,256,400]{1,2,0:T(8,128)} async-done(((f32[8,256,400]{1,2,0:T(8,128)}), f32[8,256,400]{1,2,0:T(8,128)}) %all-reduce.16.cloned.1.call-update) | async-done | bytes 3276816 | tf_op jit(solution)/shard_map/psum | solution.py:235
  853.2 21.0 %multiply_reduce_fusion.2 = (f32[400]{0:T(512)S(1)}, f32[8,1024]{1,0:T(8,128)S(1)}, f32[8,1024]{1,0:T(8,128)S(1)}, f32[400]{0:T(512)S(1)}, f32[8,1024,400]{1,2,0:T(8,128)}) fusion(f32[8,1024]{1,0:T(8,128)S(1)} %copy-done.18, f32[8,1024]{1,0:T(8,128)S(1)} %copy-done.11, f32[8,1024,400]{1,2,0:T(8,128)} %copy-done.1, f32[400]{0:T(512)S(1)} %copy-done.28, ...), kind=kLoop, calls=%fused_computation.47 | loop fusion | flops 72072416 | bytes 39460672 | tf_op jit(solution)/shard_map/reduce_sum | solution.py:43
  874.3 10.1 fusion.62
  884.5 25.9 %fusion.24 = (f32[800]{0:T(1024)S(1)}, f32[8,1024]{1,0:T(8,128)S(1)}, f32[8,1024]{1,0:T(8,128)S(1)}, f32[800]{0:T(1024)S(1)}, f32[8,1024,800]{1,2,0:T(8,128)}) fusion(f32[8,1024]{1,0:T(8,128)S(1)} %copy-done.22, f32[8,1024]{1,0:T(8,128)S(1)} %copy-done.16, bf16[8,512,800]{1,2,0:T(8,128)(2,1)S(1)} %bitcast.110, bf16[8,512,800]{1,2,0:T(8,128)(2,1)S(1)} %bitcast.118, ...), kind=kOutput, calls=%fused_computation.34 | convolution fusion | flops 5393594368 | bytes 46659072 | tf_op jit(solution)/shard_map/mre,de->mrd/dot_general | solution.py:263
  910.5 10.3 fusion.44
  920.8 28.4 %convert_reduce_fusion.1 = (f32[800]{0:T(1024)S(1)}, f32[8,1024,800]{1,2,0:T(8,128)}) fusion(bf16[8,512,800]{1,2,0:T(8,128)(2,1)} %bitcast.128, bf16[8,512,800]{1,2,0:T(8,128)(2,1)} %bitcast.131, f32[8,1024]{1,0:T(8,128)S(1)} %broadcast_multiply_fusion.6, f32[8,1024]{1,0:T(8,128)S(1)} %copy-done.16, bf16[8,512,800]{1,2,0:T(8,128)(2,1)} %bitcast.103, ...), kind=kLoop, calls=%fused_computation.12 | loop fusion | flops 111410400 | bytes 78780672 | tf_op jit(solution)/shard_map/reduce_sum | solution.py:43
  953.2 36.2 %reduce-scatter.5.cloned.1.call-done = f32[200,400]{1,0:T(8,128)} async-done(((f32[800,400]{1,0:T(8,128)}), f32[200,400]{1,0:T(8,128)}) %reduce-scatter.5.cloned.1.call-update) | async-done | bytes 320016 | tf_op jit(solution)/shard_map/reduce_scatter | solution.py:275
  989.5 17.0 %slice_bitcast_fusion = (f32[8,1,512,800]{2,3,1,0:T(8,128)}, f32[8,1,512,800]{2,3,1,0:T(8,128)}) fusion(f32[8,1024,800]{1,2,0:T(8,128)} %get-tuple-element.149), kind=kLoop, calls=%fused_computation.41 | loop fusion | bytes 52428800
  1006.6 39.9 %all-reduce.10 = (f32[800]{0:T(1024)}, f32[800]{0:T(1024)}, f32[400]{0:T(512)}, f32[400]{0:T(512)}, f32[400]{0:T(512)}, /*index=5*/f32[400]{0:T(512)}, f32[400]{0:T(512)}, f32[400]{0:T(512)}, f32[800]{0:T(1024)}) all-reduce(f32[800]{0:T(1024)S(1)} %get-tuple-element.96, ...), channel_id=1, replica_groups=mesh['rep'=8,'shard'=4] {'rep','shard'}, use_global_device_ids=true, to_apply=%region_26.27 | all-reduce | flops 4800 | bytes 38400 | tf_op jit(solution)/shard_map/psum | solution.py:270
  (214 shorter events, 139.8 us)
Async XLA Ops:
  7.2 170.1 %all-gather.4.cloned.1.call-start = ((), (), s32[]{:S(2)}) async-start(), calls=%async_computation.1 | async-start | bytes 2359296 | tf_op jit(solution)/shard_map/all_gather | solution.py:118
  7.3 34.4 %copy-start.31 = (f32[800]{0:T(1024)S(1)}, f32[800]{0:T(1024)}, u32[]{:S(2)}) copy-start(f32[800]{0:T(1024)} %param.25) | copy-start | bytes 9604
  7.3 34.3 %copy-start.38 = (f32[800]{0:T(1024)S(1)}, f32[800]{0:T(1024)}, u32[]{:S(2)}) copy-start(f32[800]{0:T(1024)} %param.26) | copy-start | bytes 9604
  75.3 40.3 %copy-start.40 = (s32[8,1,2]{0,2,1:T(2,128)S(1)}, s32[8,1,2]{0,2,1:T(2,128)}, u32[]{:S(2)}) copy-start(s32[8,1,2]{0,2,1:T(2,128)} %param.21) | copy-start | bytes 196
  75.3 40.4 %copy-start.46 = (s32[8,1,2]{0,2,1:T(2,128)S(1)}, s32[8,1,2]{0,2,1:T(2,128)}, u32[]{:S(2)}) copy-start(s32[8,1,2]{0,2,1:T(2,128)} %param.20) | copy-start | bytes 196
  75.3 40.5 %copy-start.48 = (s32[2]{0:T(128)S(1)}, s32[2]{0:T(128)}, u32[]{:S(2)}) copy-start(s32[2]{0:T(128)} %constant.85) | copy-start | bytes 28
  75.3 40.6 %copy-start.47 = (s32[2]{0:T(128)S(1)}, s32[2]{0:T(128)}, u32[]{:S(2)}) copy-start(s32[2]{0:T(128)} %constant.88) | copy-start | bytes 28
  75.3 41.9 %copy-start.14 = (f32[3,100,400]{1,2,0:T(8,128)S(1)}, f32[3,100,400]{1,2,0:T(8,128)}, u32[]{:S(2)}) copy-start(f32[3,100,400]{1,2,0:T(8,128)} %param.23) | copy-start | bytes 1440004
  75.3 42.3 %copy-start.20 = (f32[100,800]{1,0:T(8,128)S(1)}, f32[100,800]{1,0:T(8,128)}, u32[]{:S(2)}) copy-start(f32[100,800]{1,0:T(8,128)} %param.24) | copy-start | bytes 960004
  86.2 76.8 %copy-start.45 = (u32[32]{0:T(128)S(1)}, u32[32]{0:T(128)}, u32[]{:S(2)}) copy-start(u32[32]{0:T(128)} %constant.128) | copy-start | bytes 388
  87.6 83.3 %collective-permute-start = (bf16[8,32,400]{2,1,0:T(8,128)(2,1)}, bf16[8,32,400]{2,1,0:T(8,128)(2,1)}, u32[]{:S(2)}, u32[]{:S(2)}) collective-permute-start(bf16[8,32,400]{2,1,0:T(8,128)(2,1)} %copy.110), channel_id=1, source_target_pairs={{0,1},{1,2},{2,3},{4,5},{5,6},{6,7},{8,9},{9,10},{10,11},{12,13},{... | collective-permute-start | bytes 614408 | tf_op jit(solution)/shard_map/ppermute | solution.py:13
  115.5 735.0 %all-reduce.16.cloned.1.call-start = ((), (), s32[]{:S(2)}) async-start(), calls=%async_computation.2 | async-start | bytes 6553600 | tf_op jit(solution)/shard_map/psum | solution.py:235
  170.8 258.5 %copy-start.23 = (pred[8,512]{1,0:T(8,128)(4,1)}, pred[8,512]{1,0:T(8,128)(4,1)S(1)}, u32[]{:S(2)}) copy-start(pred[8,512]{1,0:T(8,128)(4,1)S(1)} %get-tuple-element.161) | copy-start | bytes 12292
  170.8 258.5 %copy-start.25 = (pred[8,512]{1,0:T(8,128)(4,1)}, pred[8,512]{1,0:T(8,128)(4,1)S(1)}, u32[]{:S(2)}) copy-start(pred[8,512]{1,0:T(8,128)(4,1)S(1)} %get-tuple-element.162) | copy-start | bytes 12292
  539.6 35.8 %copy-start.13 = (bf16[400,800,1]{1,0,2:T(8,128)(2,1)S(1)}, bf16[400,800,1]{1,0,2:T(8,128)(2,1)}, u32[]{:S(2)}) copy-start(bf16[400,800,1]{1,0,2:T(8,128)(2,1)} %reshape.261) | copy-start | bytes 1920004
  539.6 35.8 %copy-start.49 = (f32[800]{0:T(1024)S(1)}, f32[800]{0:T(1024)}, u32[]{:S(2)}) copy-start(f32[800]{0:T(1024)} %param.33) | copy-start | bytes 9604
  573.8 184.2 %collective-permute-start.2 = (f32[36,800]{1,0:T(8,128)S(1)}, f32[36,800]{1,0:T(8,128)S(1)}, u32[]{:S(2)}, u32[]{:S(2)}) collective-permute-start(f32[36,800]{1,0:T(8,128)S(1)} %slice.111), channel_id=1, source_target_pairs={{0,1},{1,2},{2,3},{4,5},{5,6},{6,7},{8,9},{9,10},{10,11},{12,13},{... | collective-permute-start | bytes 345608
  714.3 237.0 %all-reduce.18.cloned.1.call-start = ((), (), s32[]{:S(2)}) async-start(), calls=%async_computation.4 | async-start | bytes 4915200
  727.3 31.9 %collective-permute-start.1 = (bf16[8,32,400]{2,1,0:T(8,128)(2,1)S(1)}, bf16[8,32,400]{2,1,0:T(8,128)(2,1)S(1)}, u32[]{:S(2)}, u32[]{:S(2)}) collective-permute-start(bf16[8,32,400]{2,1,0:T(8,128)(2,1)S(1)} %copy.123), channel_id=1, source_target_pairs={{1,0},{2,1},{3,2},{5,4},{6,5},{7,6},{9,8},{10,9},{11,10},{13,12},{... | collective-permute-start | bytes 614408 | tf_op jit(solution)/shard_map/ppermute | solution.py:13
  739.3 250.1 %reduce-scatter.5.cloned.1.call-start = ((), (), s32[]{:S(2)}) async-start(), calls=%async_computation.3 | async-start | bytes 2048000 | tf_op jit(solution)/shard_map/reduce_scatter | solution.py:275
  750.1 103.0 %copy-start.11 = (f32[8,1024]{1,0:T(8,128)S(1)}, f32[8,1024]{1,0:T(8,128)}, u32[]{:S(2)}) copy-start(f32[8,1024]{1,0:T(8,128)} %copy-done.10) | copy-start | bytes 98308
  750.1 103.0 %copy-start.18 = (f32[8,1024]{1,0:T(8,128)S(1)}, f32[8,1024]{1,0:T(8,128)}, u32[]{:S(2)}) copy-start(f32[8,1024]{1,0:T(8,128)} %copy-done.17) | copy-start | bytes 98308
  750.1 103.0 %copy-start.28 = (f32[400]{0:T(512)S(1)}, f32[400]{0:T(512)}, u32[]{:S(2)}) copy-start(f32[400]{0:T(512)} %param.27) | copy-start | bytes 4804
  750.1 103.0 %copy-start.30 = (f32[400]{0:T(512)S(1)}, f32[400]{0:T(512)}, u32[]{:S(2)}) copy-start(f32[400]{0:T(512)} %param.28) | copy-start | bytes 4804
  750.1 103.0 %copy-start.35 = (f32[400]{0:T(512)S(1)}, f32[400]{0:T(512)}, u32[]{:S(2)}) copy-start(f32[400]{0:T(512)} %param.29) | copy-start | bytes 4804
  850.5 33.9 %slice-start.6 = ((s8[6553600]{0:T(1024)(128)(4,1)}), s8[4194304]{0:T(1024)(128)(4,1)S(1)}, s32[]{:S(2)}) async-start(s8[6553600]{0:T(1024)(128)(4,1)} %bitcast.108), calls=%async_computation.12 | async-start | bytes 8388608
  850.5 33.9 %slice-start.8 = ((s8[6553600]{0:T(1024)(128)(4,1)}), s8[4194304]{0:T(1024)(128)(4,1)S(1)}, s32[]{:S(2)}) async-start(s8[6553600]{0:T(1024)(128)(4,1)} %bitcast.116), calls=%async_computation.14 | async-start | bytes 8388608
  853.2 31.2 %slice-start.7 = ((s8[6553600]{0:T(1024)(128)(4,1)}), s8[2359296]{0:T(1024)(128)(4,1)S(1)}, s32[]{:S(2)}) async-start(s8[6553600]{0:T(1024)(128)(4,1)} %bitcast.108), calls=%async_computation.13 | async-start | bytes 4718592
  853.2 31.2 %slice-start.9 = ((s8[6553600]{0:T(1024)(128)(4,1)}), s8[2359296]{0:T(1024)(128)(4,1)S(1)}, s32[]{:S(2)}) async-start(s8[6553600]{0:T(1024)(128)(4,1)} %bitcast.116), calls=%async_computation.15 | async-start | bytes 4718592
  874.3 36.2 %slice-start.10 = ((s8[13107200]{0:T(1024)(128)(4,1)}), s8[524288]{0:T(1024)(128)(4,1)S(1)}, s32[]{:S(2)}) async-start(s8[13107200]{0:T(1024)(128)(4,1)} %bitcast.122), calls=%async_computation.16 | async-start | bytes 1048576
  884.5 26.0 %slice-start.11 = ((s8[13107200]{0:T(1024)(128)(4,1)}), s8[4194304]{0:T(1024)(128)(4,1)S(1)}, s32[]{:S(2)}) async-start(s8[13107200]{0:T(1024)(128)(4,1)} %bitcast.122), calls=%async_computation.17 | async-start | bytes 8388608
  920.8 130.5 %all-reduce.20.cloned.1.call-start = ((), (), s32[]{:S(2)}) async-start(), calls=%async_computation.5 | async-start | bytes 2842624 | tf_op jit(solution)/shard_map/psum | solution.py:279
  (40 other events, 516.4 us)
Sparse Core Ops, SparseCore 0:
  115.6 27.8 all-gather.3
  714.4 136.0 all-reduce.15
  853.0 98.1 all-reduce.17
  954.1 35.3 reduce-scatter.4
  993.4 57.8 all-reduce.19
